TPU v7x, 32 devices: a whole 2x2x4 slice. The times are simulated.
32 devices in a mesh: node: 8 (over y, x, core), shot: 4 (over z).
Axes of the slice: x: 2, y: 2, z: 4, core: 2. Of those that a mesh axis runs over, the one named last changes fastest.
Arguments:
- spectra: bfloat16 [64, 2, 512, 1024], P(None, None, 'shot', 'node'), may hold values from -6 to 6
- source_block: int32 [6], replicated, may hold values from 0 to 31
- taper_window: int32 [6, 512], replicated, may hold values from 0 to 7
Outputs:
- virtual_gathers: bfloat16 [6, 64, 2, 32, 1024], P(None, 'shot', None, None, 'node')
All inputs are finite; a program needn't handle non-finite values.
Results may differ from a plain program's by a relative error of at most 0.0047.
Values may be sent and summed in bfloat16 or wider, within the bound.
A program may use at most 128 MiB of HBM per device.

v0:
```python
import jax
import jax.numpy as jnp
from jax import lax
from jax.sharding import PartitionSpec as P

SB = 32
ROUNDS = 6
WINDOWS = 8


def from_root(x, axis, root):
    mine = lax.axis_index(axis) == root
    return lax.psum(jnp.where(mine, x, jnp.zeros_like(x)), axis)


def taper_weights(taper_windows):
    return 0.5 - 0.5 * jnp.cos(jnp.pi * (taper_windows.astype(jnp.float32) + 1.0) / (WINDOWS + 1.0))


def correlate(tapered_spectra, receiver_nodes):
    real_part = tapered_spectra[:, 0]
    imag_part = tapered_spectra[:, 1]
    real_row = jnp.stack((real_part, imag_part), axis=1)
    imag_row = jnp.stack((-imag_part, real_part), axis=1)
    operator = jnp.stack((real_row, imag_row), axis=1)
    return jnp.einsum(
        "mochn,mchr->monr", operator, receiver_nodes, preferred_element_type=jnp.float32
    )


def source_piece(spectrum_holder, block, per_device):
    offset = block % per_device * SB
    return lax.dynamic_slice_in_dim(spectrum_holder, offset, SB, 3)


def body(spectra, source_block, taper_window):
    shot_dev = spectra.shape[2]
    node_dev = spectra.shape[3]
    per_device = node_dev // SB
    shot_count = shot_dev * lax.axis_size("shot")
    scale = 1.0 / jnp.sqrt(jnp.float32(shot_count))
    shot_weights = taper_weights(taper_window)
    gather_results = []
    first_shot = lax.axis_index("shot") * shot_dev
    local_weights = lax.dynamic_slice_in_dim(shot_weights, first_shot, shot_dev, 1)
    for turn in range(ROUNDS):
        block = source_block[turn]
        piece = source_piece(spectra, block, per_device)
        received_spectra = from_root(piece, "node", block // per_device)
        tapered_spectra = (
            received_spectra.astype(jnp.float32) * local_weights[turn][:, None]
        ).astype(jnp.bfloat16)
        summed = lax.psum_scatter(
            correlate(tapered_spectra, spectra) * scale, "shot", scatter_dimension=0, tiled=True
        )
        gather_results.append(summed.astype(jnp.bfloat16))
    return jnp.stack(gather_results, axis=0)


def solution(mesh):
    in_specs = (P(None, None, "shot", "node"), P(), P())
    out_specs = P(None, "shot", None, None, "node")
    return jax.shard_map(body, mesh=mesh, in_specs=in_specs, out_specs=out_specs, check_vma=False)
```

profile of v0, /device:TPU:0, one launch (start us, length us, event | category | flops | bytes accessed | tf_op | source)
XLA Modules:
  0.0 475.1 jit_solution(9410859101491857748)
XLA Ops:
  6.5 1.6 fusion.50
  24.1 24.6 %constant_dynamic-slice_fusion = (bf16[64,2,128,32]{3,2,1,0:T(8,128)(2,1)}, bf16[64,2,128,32]{3,2,1,0:T(8,128)(2,1)}, bf16[64,2,128,32]{3,2,1,0:T(8,128)(2,1)}, ...) fusion(bf16[64,2,128,128]{3,2,1,0:T(8,128)(2,1)} %param.3, ...), kind=kLoop, calls=%fused_computation.67 | loop fusion | bytes 12582936 | tf_op jit(solution)/shard_map/dynamic_slice | solution.py:33
  48.7 4.6 copy.28
  53.2 4.6 copy.27
  57.8 4.6 copy.26
  62.4 3.6 copy.25
  66.0 3.6 copy.24
  69.5 3.6 copy.23
  73.1 1.2 broadcast_select_fusion
  74.3 0.4 copy-done.7
  74.7 1.0 broadcast_select_fusion.1
  75.8 1.1 broadcast_select_fusion.2
  76.8 1.0 broadcast_select_fusion.3
  77.8 1.1 broadcast_select_fusion.4
  78.9 1.0 broadcast_select_fusion.5
  80.0 0.0 reduce-scatter.7.cloned.1.call-start
  80.0 0.7 fusion.48
  80.8 107.7 %all-reduce.3.cloned.1.call-done = (bf16[64,2,128,32]{2,3,1,0:T(8,128)(2,1)}, bf16[64,2,128,32]{2,3,1,0:T(8,128)(2,1)}, bf16[64,2,128,32]{2,3,1,0:T(8,128)(2,1)}...) async-done(((bf16[64,2,128,32]{2,3,1,0:T(8,128)(2,1)}, bf16[64,2,128,32]{2,3,1,0:T(8,128)(2,1)}, ...) | async-done | bytes 6291472 | tf_op jit(solution)/shard_map/psum | solution.py:13
  188.5 2.0 multiply_convert_fusion.4
  190.5 0.1 slice_negate_fusion.5
  190.6 0.1 maximum_bitcast_fusion
  190.7 2.0 copy-done
  192.7 2.3 bitcast_multiply_fusion.5
  195.0 0.0 reduce-scatter.9.cloned.1.call-start
  195.0 0.1 slice_negate_fusion.4
  195.2 0.1 maximum_bitcast_fusion.1
  195.3 2.0 copy-done.1
  197.2 2.2 bitcast_multiply_fusion.4
  199.5 0.0 reduce-scatter.11.cloned.1.call-start
  199.5 1.1 copy-done.10
  200.7 0.3 copy-done.11
  201.0 0.4 multiply_convert_fusion.2
  201.5 0.1 slice_negate_fusion.3
  201.6 0.1 maximum_bitcast_fusion.2
  201.7 2.0 copy-done.2
  203.7 2.3 bitcast_multiply_fusion.3
  206.0 0.1 slice_negate_fusion.2
  206.1 0.1 maximum_bitcast_fusion.3
  206.3 2.0 copy-done.3
  208.2 2.3 bitcast_multiply_fusion.2
  210.6 0.2 reduce-scatter.15.cloned.1.call-start
  210.8 1.0 copy-done.8
  211.8 0.3 copy-done.9
  212.1 0.4 multiply_convert_fusion
  212.6 0.1 slice_negate_fusion.1
  212.7 0.1 maximum_bitcast_fusion.4
  212.8 2.0 copy-done.4
  214.8 2.3 bitcast_multiply_fusion.1
  217.2 0.1 slice_negate_fusion
  217.3 0.1 maximum_bitcast_fusion.5
  217.4 2.0 copy-done.5
  219.4 2.3 bitcast_multiply_fusion
  221.7 17.4 %reduce-scatter.7.cloned.1.call-done = f32[16,2,32,128]{3,2,1,0:T(8,128)} async-done(((f32[64,2,32,128]{3,2,1,0:T(8,128)}), f32[16,2,32,128]{3,2,1,0:T(8,128)}) %reduce-scatter.7.cloned.1.call-update) | async-done | bytes 524304 | tf_op jit(solution)/shard_map/reduce_scatter | solution.py:53
  239.1 1.1 bitcast_dynamic-update-slice_fusion.5
  240.2 44.4 %reduce-scatter.9.cloned.1.call-done = f32[16,2,32,128]{3,2,1,0:T(8,128)} async-done(((f32[64,2,32,128]{3,2,1,0:T(8,128)}), f32[16,2,32,128]{3,2,1,0:T(8,128)}) %reduce-scatter.9.cloned.1.call-update) | async-done | bytes 524304 | tf_op jit(solution)/shard_map/reduce_scatter | solution.py:53
  284.6 1.1 bitcast_dynamic-update-slice_fusion.4
  285.7 44.4 %reduce-scatter.11.cloned.1.call-done = f32[16,2,32,128]{3,2,1,0:T(8,128)} async-done(((f32[64,2,32,128]{3,2,1,0:T(8,128)}), f32[16,2,32,128]{3,2,1,0:T(8,128)}) %reduce-scatter.11.cloned.1.call-update) | async-done | bytes 524304 | tf_op jit(solution)/shard_map/reduce_scatter | solution.py:53
  330.1 1.1 bitcast_dynamic-update-slice_fusion.3
  331.2 44.3 %reduce-scatter.13.cloned.1.call-done = f32[16,2,32,128]{3,2,1,0:T(8,128)} async-done(((f32[64,2,32,128]{3,2,1,0:T(8,128)}), f32[16,2,32,128]{3,2,1,0:T(8,128)}) %reduce-scatter.13.cloned.1.call-update) | async-done | bytes 524304 | tf_op jit(solution)/shard_map/reduce_scatter | solution.py:53
  375.5 1.1 bitcast_dynamic-update-slice_fusion.2
  376.6 44.4 %reduce-scatter.15.cloned.1.call-done = f32[16,2,32,128]{3,2,1,0:T(8,128)} async-done(((f32[64,2,32,128]{3,2,1,0:T(8,128)}), f32[16,2,32,128]{3,2,1,0:T(8,128)}) %reduce-scatter.15.cloned.1.call-update) | async-done | bytes 524304 | tf_op jit(solution)/shard_map/reduce_scatter | solution.py:53
  420.9 1.1 bitcast_dynamic-update-slice_fusion.1
  422.0 44.4 %reduce-scatter.17.cloned.1.call-done = f32[16,2,32,128]{3,2,1,0:T(8,128)} async-done(((f32[64,2,32,128]{3,2,1,0:T(8,128)}), f32[16,2,32,128]{3,2,1,0:T(8,128)}) %reduce-scatter.17.cloned.1.call-update) | async-done | bytes 524304 | tf_op jit(solution)/shard_map/reduce_scatter | solution.py:53
  466.4 1.8 bitcast_dynamic-update-slice_fusion
  (26 shorter events, 0.3 us)
Async XLA Ops:
  6.5 182.0 %all-reduce.3.cloned.1.call-start = ((), (), s32[]{:S(2)}) async-start(), calls=%async_computation.12 | async-start | bytes 12582912 | tf_op jit(solution)/shard_map/psum | solution.py:13
  73.1 1.6 copy-start.7
  73.1 2.6 copy-start.6
  80.0 159.1 %reduce-scatter.7.cloned.1.call-start = ((), (), s32[]{:S(2)}) async-start(), calls=%async_computation.6 | async-start | bytes 2621440 | tf_op jit(solution)/shard_map/reduce_scatter | solution.py:53
  190.5 2.2 copy-start
  195.0 89.7 %reduce-scatter.9.cloned.1.call-start = ((), (), s32[]{:S(2)}) async-start(), calls=%async_computation.7 | async-start | bytes 2621440 | tf_op jit(solution)/shard_map/reduce_scatter | solution.py:53
  195.0 2.2 copy-start.1
  199.5 1.2 copy-start.10
  199.5 1.5 copy-start.11
  199.5 130.6 %reduce-scatter.11.cloned.1.call-start = ((), (), s32[]{:S(2)}) async-start(), calls=%async_computation.8 | async-start | bytes 2621440 | tf_op jit(solution)/shard_map/reduce_scatter | solution.py:53
  201.4 2.2 copy-start.2
  206.0 169.5 %reduce-scatter.13.cloned.1.call-start = ((), (), s32[]{:S(2)}) async-start(), calls=%async_computation.9 | async-start | bytes 2621440 | tf_op jit(solution)/shard_map/reduce_scatter | solution.py:53
  206.0 2.2 copy-start.3
  210.6 1.2 copy-start.8
  210.6 1.6 copy-start.9
  210.6 210.3 %reduce-scatter.15.cloned.1.call-start = ((), (), s32[]{:S(2)}) async-start(), calls=%async_computation.10 | async-start | bytes 2621440 | tf_op jit(solution)/shard_map/reduce_scatter | solution.py:53
  212.6 2.2 copy-start.4
  217.2 249.3 %reduce-scatter.17.cloned.1.call-start = ((), (), s32[]{:S(2)}) async-start(), calls=%async_computation.11 | async-start | bytes 2621440 | tf_op jit(solution)/shard_map/reduce_scatter | solution.py:53
  217.2 2.2 copy-start.5
  422.0 44.4 %copy-start.12 = (bf16[6,16,2,32,128]{4,3,2,1,0:T(8,128)(2,1)}, bf16[6,16,2,32,128]{4,3,2,1,0:T(8,128)(2,1)S(1)}, u32[]{:S(2)}) copy-start(bf16[6,16,2,32,128]{4,3,2,1,0:T(8,128)(2,1)S(1)} %bitcast_dynamic-update-slice_fusion.1) | copy-start | bytes 4718596
Sparse Core Ops, SparseCore 0:
  80.1 108.3 all-reduce.2
  195.1 43.9 reduce-scatter.6
  241.4 43.1 reduce-scatter.8
  286.9 43.1 reduce-scatter.10
  332.2 43.1 reduce-scatter.12
  377.7 43.1 reduce-scatter.14
  423.2 43.1 reduce-scatter.16
where the time goes:
time: 477 us; the launch traced here: 475 us
  waiting for transfers between devices  347 us (73%)
  local copies, waits for them, and re-layouts  65.7 us (14%)
  between operations  29.7 us (6%)
  other arithmetic  18.4 us (4%)
  matrix products  13.7 us (3%)
    reduce_scatter x6, waiting for transfers between devices, body(): lax.psum_scatter(correlate(tapered_spectra, spectra) * scale, 'shot', sca...  239 us
    psum x1, waiting for transfers between devices, from_root(): return lax.psum(jnp.where(mine, x, jnp.zeros_like(x)), axis)  108 us
    unnamed x32, local copies, waits for them, and re-layouts  39.6 us
    dynamic_slice x1, local copies, waits for them, and re-layouts, source_piece(): return lax.dynamic_slice_in_dim(spectrum_holder, offset, SB, 3)  24.6 us
    dot_general x6, matrix products, correlate(): jnp.einsum('mochn,mchr->monr', operator, receiver_nodes, preferred_elemen...  13.7 us
  transfers between devices with their start and end apart: 7, of which 7 were waited for; matrix products, arithmetic and copies ran while one was open for 4% of the time, Pallas kernels for 0%

commit v1 on v0

v1 whole, which is shorter than its diff:
```python
import functools

import jax
import jax.numpy as jnp
from jax import lax
from jax.experimental import pallas as pl
from jax.experimental.pallas import tpu as pltpu
from jax.sharding import PartitionSpec as P

SB = 32
WINDOWS = 8
MESH = pl.DeviceIdType.MESH
AHEAD = 4


def taper_weights(taper_windows):
    return 0.5 - 0.5 * jnp.cos(jnp.pi * (taper_windows.astype(jnp.float32) + 1.0) / (WINDOWS + 1.0))


def kernel(
    nodes, groups, stages, scale,
    sel_ref, weight_ref, x_ref, out_ref,
    recv, part, full, *rest,
):
    levels = nodes.bit_length() - 1
    land = rest[:levels]
    own_sem, zs, zr, rs, rr, gs, gr = rest[levels:]
    me = lax.axis_index("node")
    group = lax.axis_index("shot")
    f_dev = recv.shape[0]
    fs = f_dev // stages
    rows = sel_ref.shape[0]
    shots = part.shape[-1]
    unit = part.shape[2]
    per = rows // unit
    rounds = rows // SB
    receivers = recv.shape[-1]

    def peer_at(stride):
        bit = (me // stride) % 2
        return bit, me + stride * (1 - 2 * bit)

    def hop(level, j):
        bit, peer = peer_at(2**level)
        if level:
            bit_odd, peer_odd = peer_at(2 ** (levels - level))
            odd = j % 2
            bit = bit + odd * (bit_odd - bit)
            peer = peer + odd * (peer_odd - peer)
        return bit, peer

    def offset(level, j):
        at = 0
        for lower in range(level):
            at = at + hop(lower, j)[0] * (nodes >> (lower + 1))
        return at

    def spectra_copy(j, d):
        to = (group + d) % groups
        return pltpu.make_async_remote_copy(
            src_ref=x_ref.at[pl.ds(to * f_dev + j * fs, fs)],
            dst_ref=recv.at[pl.ds(j * fs, fs), :, group],
            send_sem=zs.at[j, d - 1],
            recv_sem=zr.at[j, d - 1],
            device_id=(me, to),
            device_id_type=MESH,
        )

    def spectra_arrival(j, d):
        source = (group + groups - d) % groups
        place = recv.at[pl.ds(j * fs, fs), :, source]
        return pltpu.make_async_remote_copy(
            src_ref=place,
            dst_ref=place,
            send_sem=zs.at[j, d - 1],
            recv_sem=zr.at[j, d - 1],
            device_id=(me, source),
            device_id_type=MESH,
        )

    def reduce_copy(level, j):
        bit, peer = hop(level, j)
        size = nodes >> (level + 1)
        return pltpu.make_async_remote_copy(
            src_ref=part.at[j, pl.ds(offset(level, j) + (1 - bit) * size, size)],
            dst_ref=land[level].at[j],
            send_sem=rs.at[level, j],
            recv_sem=rr.at[level, j],
            device_id=(peer, group),
            device_id_type=MESH,
        )

    def gather_copy(level, j, arrival=False):
        bit, peer = hop(level, j)
        size = nodes >> (level + 1)
        half = 1 - bit if arrival else bit
        place = full.at[j, pl.ds(offset(level, j) + half * size, size)]
        return pltpu.make_async_remote_copy(
            src_ref=place,
            dst_ref=place,
            send_sem=gs.at[level, j],
            recv_sem=gr.at[level, j],
            device_id=(peer, group),
            device_id_type=MESH,
        )

    own_copy = pltpu.make_async_copy(
        x_ref.at[pl.ds(group * f_dev, f_dev)], recv.at[:, :, group], own_sem
    )
    own_copy.start()

    barrier = pltpu.get_barrier_semaphore()
    for level in range(levels):
        pl.semaphore_signal(barrier, inc=1, device_id=(peer_at(2**level)[1], group), device_id_type=MESH)
    for d in range(1, groups):
        pl.semaphore_signal(barrier, inc=1, device_id=(me, (group + d) % groups), device_id_type=MESH)
    pl.semaphore_wait(barrier, levels + groups - 1)

    def send_spectra(j):
        for d in range(1, groups):
            spectra_copy(j, d).start()

    for j in range(min(AHEAD, stages)):
        send_spectra(j)
    own_copy.wait()

    def select(j):
        for d in range(1, groups):
            spectra_arrival(j, d).wait_recv()

        @pl.when(j + AHEAD < stages)
        def _():
            send_spectra(j + AHEAD)

        for f in range(fs):
            for c in range(2):
                block = recv[j * fs + f, c].reshape(shots, receivers)
                picked = lax.dot_general(
                    sel_ref[...], block, (((1,), (1,)), ((), ())),
                    preferred_element_type=jnp.float32,
                ).reshape(rounds, SB, shots)
                tapered = (picked * weight_ref[...][:, None, :]).astype(jnp.bfloat16)
                part[j, pl.ds((f * 2 + c) * per, per)] = tapered.reshape(per, unit, shots)
        reduce_copy(0, j).start()

    def reduce(level, j):
        reduce_copy(level, j).wait_recv()
        bit, _ = hop(level, j)
        size = nodes >> (level + 1)
        kept = pl.ds(offset(level, j) + bit * size, size)
        total = part[j, kept] + land[level][j]
        if level + 1 < levels:
            part[j, kept] = total
            reduce_copy(level + 1, j).start()
        else:
            full[j, kept] = total
            gather_copy(level, j).start()

    def correlate(j):
        for f in range(fs):
            first = full[j, pl.ds(2 * f * per, per)].reshape(rows, shots)
            second = full[j, pl.ds((2 * f + 1) * per, per)].reshape(rows, shots)
            both = jnp.concatenate(
                [recv[j * fs + f, c].reshape(shots, receivers) for c in range(2)], axis=1
            )
            by_first = jnp.dot(first, both, preferred_element_type=jnp.float32)
            by_second = jnp.dot(second, both, preferred_element_type=jnp.float32)
            real = (by_first[:, :receivers] + by_second[:, receivers:]) * scale
            imag = (by_first[:, receivers:] - by_second[:, :receivers]) * scale
            out_ref[:, j * fs + f, 0] = real.reshape(rounds, SB, receivers).astype(jnp.bfloat16)
            out_ref[:, j * fs + f, 1] = imag.reshape(rounds, SB, receivers).astype(jnp.bfloat16)

    def gather(level, j):
        gather_copy(level, j, arrival=True).wait_recv()
        if level:
            gather_copy(level - 1, j).start()
        else:
            correlate(j)

    steps = [select]
    steps += [functools.partial(reduce, level) for level in range(levels)]
    steps += [functools.partial(gather, level) for level in reversed(range(levels))]

    @pl.loop(0, stages + len(steps) - 1)
    def _(tick):
        for place in reversed(range(len(steps))):
            j = tick - place
            pl.when((j >= 0) & (j < stages))(functools.partial(steps[place], j))

    @pl.loop(0, stages)
    def _(j):
        for d in range(1, groups):
            spectra_copy(j, d).wait_send()
        for level in range(levels):
            reduce_copy(level, j).wait_send()
            gather_copy(level, j).wait_send()


def body(spectra, source_block, taper_window):
    f_all, parts, shot_dev, node_dev = spectra.shape
    nodes = lax.axis_size("node")
    groups = lax.axis_size("shot")
    levels = nodes.bit_length() - 1
    rounds = source_block.shape[0]
    f_dev = f_all // groups
    shots = shot_dev * groups
    rows = rounds * SB
    fs = max(2, nodes // 8)
    stages = f_dev // fs
    unit = fs * parts * rows // nodes
    scale = 1.0 / float(shots) ** 0.5

    first = lax.axis_index("node") * node_dev
    picked = source_block[:, None] * SB + jnp.arange(SB, dtype=jnp.int32)[None, :] - first
    sel = (picked.reshape(rows, 1) == jnp.arange(node_dev, dtype=jnp.int32)[None, :]).astype(jnp.bfloat16)
    weights = taper_weights(taper_window)

    bf = jnp.bfloat16
    dma = pltpu.SemaphoreType.DMA
    return pl.pallas_call(
        functools.partial(kernel, nodes, groups, stages, scale),
        out_shape=jax.ShapeDtypeStruct((rounds, f_dev, parts, SB, node_dev), bf),
        in_specs=[
            pl.BlockSpec(memory_space=pltpu.VMEM),
            pl.BlockSpec(memory_space=pltpu.VMEM),
            pl.BlockSpec(memory_space=pl.ANY),
        ],
        out_specs=pl.BlockSpec(memory_space=pltpu.VMEM),
        scratch_shapes=[
            pltpu.VMEM((f_dev, parts, groups, shot_dev, node_dev), bf),
            pltpu.VMEM((stages, nodes, unit, shots), bf),
            pltpu.VMEM((stages, nodes, unit, shots), bf),
            *[pltpu.VMEM((stages, nodes >> (level + 1), unit, shots), bf) for level in range(levels)],
            dma,
            dma((stages, groups - 1)),
            dma((stages, groups - 1)),
            dma((levels, stages)),
            dma((levels, stages)),
            dma((levels, stages)),
            dma((levels, stages)),
        ],
        compiler_params=pltpu.CompilerParams(
            collective_id=0, has_side_effects=True, vmem_limit_bytes=48 * 1024 * 1024
        ),
        cost_estimate=pl.CostEstimate(
            flops=2 * 5 * f_dev * rows * shots * node_dev * 2, bytes_accessed=spectra.size * 4, transcendentals=0
        ),
    )(sel, weights, spectra)


def solution(mesh):
    in_specs = (P(None, None, "shot", "node"), P(), P())
    out_specs = P(None, "shot", None, None, "node")
    return jax.shard_map(body, mesh=mesh, in_specs=in_specs, out_specs=out_specs, check_vma=False)
```

time: 477 us -> 136 us (0.29)
  the two profiles are of different devices: /device:TPU:0 before, /device:TPU:25 now
where the time goes in v1:
time: 136 us
  Pallas kernels  131 us (96%)
  local copies, waits for them, and re-layouts  3.41 us (3%)
  other arithmetic  1.61 us (1%)
    pallas_call x1, Pallas kernels, body(): pl.pallas_call(functools.partial(kernel, nodes, groups, stages, scale), o...  131 us
    unnamed x3, local copies, waits for them, and re-layouts  3.33 us

profile of v1, /device:TPU:25, one launch (start us, length us, event | category | flops | bytes accessed | tf_op | source)
XLA Modules:
  0.0 136.0 jit_solution(1713005495950301836)
XLA Ops:
  0.0 0.7 broadcast_multiply_fusion
  0.7 0.1 add_subtract_fusion
  0.7 0.1 sub.18
  0.8 0.8 multiply_subtract_fusion.weight_ref
  1.6 0.1 fusion.sel_ref
  1.7 0.0 copy-start
  1.7 2.2 %copy-done = bf16[64,2,128,128]{3,2,1,0:T(8,128)(2,1)S(1)} copy-done((bf16[64,2,128,128]{3,2,1,0:T(8,128)(2,1)S(1)}, bf16[64,2,128,128]{3,2,1,0:T(8,128)(2,1)}, u32[]{:S(2)}) %copy-start) | copy-done | bytes 4194328
  3.9 131.0 %shard_map.37 = bf16[6,16,2,32,128]{4,3,2,1,0:T(8,128)(2,1)S(1)} custom-call(bf16[192,128]{1,0:T(8,128)(2,1)S(1)} %fusion.sel_ref, f32[6,512]{1,0:T(8,128)S(1)} %multiply_subtract_fusion.weight_ref, bf16[64,2,128,128]{3,2,1,0:T(8,128)(2,1)S(1)} %copy-done), custom_call_target="tpu_custom_call" | custom-call | flops 4026531840 | bytes 8388608 | tf_op jit(solution)/shard_map/pallas_call | solution.py:220
  134.9 1.1 copy.5
Async XLA Ops:
  1.7 2.2 %copy-start = (bf16[64,2,128,128]{3,2,1,0:T(8,128)(2,1)S(1)}, bf16[64,2,128,128]{3,2,1,0:T(8,128)(2,1)}, u32[]{:S(2)}) copy-start(bf16[64,2,128,128]{3,2,1,0:T(8,128)(2,1)} %x_ref.1) | copy-start | bytes 12582916

commit v2 on v1

--- a/solution.py
+++ b/solution.py
@@ -205,7 +205,7 @@
     f_dev = f_all // groups
     shots = shot_dev * groups
     rows = rounds * SB
-    fs = max(2, nodes // 8)
+    fs = max(1, nodes // 8)
     stages = f_dev // fs
     unit = fs * parts * rows // nodes
     scale = 1.0 / float(shots) ** 0.5
@@ -240,7 +240,7 @@
             dma((levels, stages)),
         ],
         compiler_params=pltpu.CompilerParams(
-            collective_id=0, has_side_effects=True, vmem_limit_bytes=48 * 1024 * 1024
+            collective_id=0, has_side_effects=True, vmem_limit_bytes=60 * 1024 * 1024
         ),
         cost_estimate=pl.CostEstimate(
             flops=2 * 5 * f_dev * rows * shots * node_dev * 2, bytes_accessed=spectra.size * 4, transcendentals=0

time: 136 us -> 137 us (level)
    unnamed x3 -> x1, local copies, waits for them, and re-layouts: 3.33 us -> 3.02 us
where the time goes in v2:
time: 137 us
  Pallas kernels  131 us (96%)
  local copies, waits for them, and re-layouts  3.1 us (2%)
  other arithmetic  2.84 us (2%)
    pallas_call x1, Pallas kernels, body(): pl.pallas_call(functools.partial(kernel, nodes, groups, stages, scale), o...  131 us
    unnamed x1, local copies, waits for them, and re-layouts  3.02 us

profile of v2, /device:TPU:25, one launch (start us, length us, event | category | flops | bytes accessed | tf_op | source)
XLA Modules:
  0.0 137.1 jit_solution(8070816464502240470)
XLA Ops:
  0.0 0.7 broadcast_multiply_fusion
  0.7 0.1 add_subtract_fusion
  0.7 0.1 sub.18
  0.8 1.4 %multiply_subtract_fusion.weight_ref = f32[6,512]{1,0:T(8,128)} fusion(s32[6,512]{1,0:T(8,128)} %param.5), kind=kLoop, calls=%fused_computation.2 | loop fusion | flops 15360 | bytes 24576 | tf_op jit(solution)/shard_map/sub | solution.py:17
  2.2 0.7 fusion.sel_ref
  2.9 131.2 %shard_map.37 = bf16[6,16,2,32,128]{4,3,2,1,0:T(8,128)(2,1)} custom-call(bf16[192,128]{1,0:T(8,128)(2,1)} %fusion.sel_ref, f32[6,512]{1,0:T(8,128)} %multiply_subtract_fusion.weight_ref, bf16[64,2,128,128]{3,2,1,0:T(8,128)(2,1)} %x_ref.1), custom_call_target="tpu_custom_call" | custom-call | flops 4026531840 | bytes 8388608 | tf_op jit(solution)/shard_map/pallas_call | solution.py:220
  134.1 3.0 %copy.5 = bf16[6,16,2,32,128]{4,3,2,1,0:T(8,128)(2,1)} copy(bf16[6,16,2,32,128]{4,3,2,1,0:T(8,128)(2,1)} %shard_map.37) | data formatting | bytes 3145728

commit v3 on v2

--- a/solution.py
+++ b/solution.py
@@ -11,6 +11,7 @@
 WINDOWS = 8
 MESH = pl.DeviceIdType.MESH
 AHEAD = 4
+SPACING = 2
 
 
 def taper_weights(taper_windows):
@@ -181,10 +182,10 @@
     steps += [functools.partial(reduce, level) for level in range(levels)]
     steps += [functools.partial(gather, level) for level in reversed(range(levels))]
 
-    @pl.loop(0, stages + len(steps) - 1)
+    @pl.loop(0, stages + SPACING * (len(steps) - 1))
     def _(tick):
         for place in reversed(range(len(steps))):
-            j = tick - place
+            j = tick - SPACING * place
             pl.when((j >= 0) & (j < stages))(functools.partial(steps[place], j))
 
     @pl.loop(0, stages)
@@ -240,7 +241,7 @@
             dma((levels, stages)),
         ],
         compiler_params=pltpu.CompilerParams(
-            collective_id=0, has_side_effects=True, vmem_limit_bytes=60 * 1024 * 1024
+            collective_id=0, has_side_effects=True, vmem_limit_bytes=48 * 1024 * 1024
         ),
         cost_estimate=pl.CostEstimate(
             flops=2 * 5 * f_dev * rows * shots * node_dev * 2, bytes_accessed=spectra.size * 4, transcendentals=0

time: 137 us -> 128 us (0.934)
  the two profiles are of different devices: /device:TPU:25 before, /device:TPU:0 now
where the time goes in v3:
time: 128 us; the launch traced here: 125 us
  Pallas kernels  120 us (94%)
  local copies, waits for them, and re-layouts  3.41 us (3%)
  other arithmetic  1.61 us (1%)
    pallas_call x1, Pallas kernels, body(): pl.pallas_call(functools.partial(kernel, nodes, groups, stages, scale), o...  120 us
    unnamed x3, local copies, waits for them, and re-layouts  3.33 us

profile of v3, /device:TPU:0, one launch (start us, length us, event | category | flops | bytes accessed | tf_op | source)
XLA Modules:
  0.0 125.2 jit_solution(12143239623263644571)
XLA Ops:
  0.0 0.7 broadcast_multiply_fusion
  0.7 0.1 add_subtract_fusion
  0.7 0.1 sub.18
  0.8 0.8 multiply_subtract_fusion.weight_ref
  1.6 0.1 fusion.sel_ref
  1.7 0.0 copy-start
  1.7 2.2 %copy-done = bf16[64,2,128,128]{3,2,1,0:T(8,128)(2,1)S(1)} copy-done((bf16[64,2,128,128]{3,2,1,0:T(8,128)(2,1)S(1)}, bf16[64,2,128,128]{3,2,1,0:T(8,128)(2,1)}, u32[]{:S(2)}) %copy-start) | copy-done | bytes 4194328
  3.9 120.1 %shard_map.37 = bf16[6,16,2,32,128]{4,3,2,1,0:T(8,128)(2,1)S(1)} custom-call(bf16[192,128]{1,0:T(8,128)(2,1)S(1)} %fusion.sel_ref, f32[6,512]{1,0:T(8,128)S(1)} %multiply_subtract_fusion.weight_ref, bf16[64,2,128,128]{3,2,1,0:T(8,128)(2,1)S(1)} %copy-done), custom_call_target="tpu_custom_call" | custom-call | flops 4026531840 | bytes 8388608 | tf_op jit(solution)/shard_map/pallas_call | solution.py:221
  124.0 1.1 copy.5
Async XLA Ops:
  1.7 2.2 %copy-start = (bf16[64,2,128,128]{3,2,1,0:T(8,128)(2,1)S(1)}, bf16[64,2,128,128]{3,2,1,0:T(8,128)(2,1)}, u32[]{:S(2)}) copy-start(bf16[64,2,128,128]{3,2,1,0:T(8,128)(2,1)} %x_ref.1) | copy-start | bytes 12582916

commit v4 on v3

v4 whole, which is shorter than its diff:
```python
import functools

import jax
import jax.numpy as jnp
from jax import lax
from jax.experimental import pallas as pl
from jax.experimental.pallas import tpu as pltpu
from jax.sharding import PartitionSpec as P

SB = 32
WINDOWS = 8
MESH = pl.DeviceIdType.MESH
AHEAD = 6
SPACING = 2
LATER = 5


def taper_weights(taper_windows):
    return 0.5 - 0.5 * jnp.cos(jnp.pi * (taper_windows.astype(jnp.float32) + 1.0) / (WINDOWS + 1.0))


def kernel(
    nodes, groups, stages, scale,
    sel_ref, weight_ref, x_ref, out_ref,
    recv, part, full, acc, out_part, in_part, *rest,
):
    levels = nodes.bit_length() - 1
    land = rest[:levels]
    own_sem, zs, zr, rs, rr, gs, gr, ps, pr = rest[levels:]
    me = lax.axis_index("node")
    group = lax.axis_index("shot")
    half = groups // 2
    side, rank = group // half, group % half
    counterpart = (1 - side) * half + rank
    fs = recv.shape[1]
    f_dev = stages * fs
    halves = stages // 2
    mid = part.shape[-1] // 2
    rows = sel_ref.shape[0]
    shots = part.shape[-1]
    unit = part.shape[2]
    per = rows // unit
    rounds = rows // SB
    receivers = recv.shape[-1]

    def peer_at(stride):
        bit = (me // stride) % 2
        return bit, me + stride * (1 - 2 * bit)

    def hop(level, j):
        bit, peer = peer_at(2**level)
        if level:
            bit_odd, peer_odd = peer_at(2 ** (levels - level))
            odd = j % 2
            bit = bit + odd * (bit_odd - bit)
            peer = peer + odd * (peer_odd - peer)
        return bit, peer

    def offset(level, j):
        at = 0
        for lower in range(level):
            at = at + hop(lower, j)[0] * (nodes >> (lower + 1))
        return at

    def is_split(j):
        return (j == 0) | ((j % 2 == 1) & (j < stages - 1))

    def split_first(j):
        return (j + 1) // 2 * fs

    def whole_first(j):
        return (halves + (j + 1) // 2 - 1) * fs

    def frequencies(owner, first):
        return x_ref.at[pl.ds(owner * f_dev + first, fs)]

    def send(j, number, source, slot, to):
        return pltpu.make_async_remote_copy(
            src_ref=source,
            dst_ref=recv.at[j, :, :, slot],
            send_sem=zs.at[j, number],
            recv_sem=zr.at[j, number],
            device_id=(me, to),
            device_id_type=MESH,
        )

    def whole_sends(j):
        first = whole_first(j)
        out = []
        for d in range(1, groups):
            to = (group + d) % groups
            out.append(send(j, d - 1, frequencies(to, first), group, to))
        return out

    def whole_arrivals(j):
        out = []
        for d in range(1, groups):
            source = (group + groups - d) % groups
            out.append(send(j, d - 1, recv.at[j, :, :, source], source, source))
        return out

    def split_sends(j):
        first = split_first(j)
        out = []
        for d in range(1, half):
            to = (rank + d) % half
            for other in range(2):
                owner = (side + other * (1 - 2 * side)) * half + to
                out.append(
                    send(j, 2 * (d - 1) + other, frequencies(owner, first), other * half + rank, side * half + to)
                )
        return out

    def split_arrivals(j):
        out = []
        for d in range(1, half):
            source = (rank + half - d) % half
            for other in range(2):
                place = other * half + source
                out.append(send(j, 2 * (d - 1) + other, recv.at[j, :, :, place], place, side * half + source))
        return out

    def whole_own(j):
        return [
            pltpu.make_async_copy(frequencies(group, whole_first(j)), recv.at[j, :, :, group], own_sem.at[j, 0])
        ]

    def split_own(j):
        return [
            pltpu.make_async_copy(frequencies(group, split_first(j)), recv.at[j, :, :, rank], own_sem.at[j, 0]),
            pltpu.make_async_copy(
                frequencies(counterpart, split_first(j)), recv.at[j, :, :, half + rank], own_sem.at[j, 1]
            ),
        ]

    def partial_copy(j):
        place = pl.ds(split_first(j), fs)
        return pltpu.make_async_remote_copy(
            src_ref=out_part.at[place],
            dst_ref=in_part.at[place],
            send_sem=ps.at[j],
            recv_sem=pr.at[j],
            device_id=(me, counterpart),
            device_id_type=MESH,
        )

    def by_kind(j, on_split, on_whole):
        split = is_split(j)
        pl.when(split)(functools.partial(on_split, j))
        pl.when(jnp.logical_not(split))(functools.partial(on_whole, j))

    def reduce_copy(level, j):
        bit, peer = hop(level, j)
        size = nodes >> (level + 1)
        return pltpu.make_async_remote_copy(
            src_ref=part.at[j, pl.ds(offset(level, j) + (1 - bit) * size, size)],
            dst_ref=land[level].at[j],
            send_sem=rs.at[level, j],
            recv_sem=rr.at[level, j],
            device_id=(peer, group),
            device_id_type=MESH,
        )

    def gather_copy(level, j, arrival=False):
        bit, peer = hop(level, j)
        size = nodes >> (level + 1)
        side_at = 1 - bit if arrival else bit
        place = full.at[j, pl.ds(offset(level, j) + side_at * size, size)]
        return pltpu.make_async_remote_copy(
            src_ref=place,
            dst_ref=place,
            send_sem=gs.at[level, j],
            recv_sem=gr.at[level, j],
            device_id=(peer, group),
            device_id_type=MESH,
        )

    barrier = pltpu.get_barrier_semaphore()
    for level in range(levels):
        pl.semaphore_signal(barrier, inc=1, device_id=(peer_at(2**level)[1], group), device_id_type=MESH)
    for d in range(1, groups):
        pl.semaphore_signal(barrier, inc=1, device_id=(me, (group + d) % groups), device_id_type=MESH)
    pl.semaphore_wait(barrier, levels + groups - 1)

    def start_split(j):
        for copy in split_sends(j) + split_own(j):
            copy.start()

    def start_whole(j):
        for copy in whole_sends(j) + whole_own(j):
            copy.start()

    @pl.loop(0, min(AHEAD, stages))
    def _(j):
        by_kind(j, start_split, start_whole)

    def pick(j, kind):
        for f in range(fs):
            for c in range(2):
                block = recv[j, f, c].reshape(shots, receivers)
                picked = lax.dot_general(
                    sel_ref[...], block, (((1,), (1,)), ((), ())),
                    preferred_element_type=jnp.float32,
                ).reshape(rounds, SB, shots)
                tapered = (picked * weight_ref[kind][:, None, :]).astype(jnp.bfloat16)
                part[j, pl.ds((f * 2 + c) * per, per)] = tapered.reshape(per, unit, shots)

    def select_split(j):
        for copy in split_own(j):
            copy.wait()
        for copy in split_arrivals(j):
            copy.wait_recv()
        pick(j, 1)

    def select_whole(j):
        for copy in whole_own(j):
            copy.wait()
        for copy in whole_arrivals(j):
            copy.wait_recv()
        pick(j, 0)

    def select(j):
        pl.when(j + AHEAD < stages)(lambda: by_kind(j + AHEAD, start_split, start_whole))
        by_kind(j, select_split, select_whole)
        reduce_copy(0, j).start()

    def reduce(level, j):
        reduce_copy(level, j).wait_recv()
        bit, _ = hop(level, j)
        size = nodes >> (level + 1)
        kept = pl.ds(offset(level, j) + bit * size, size)
        total = part[j, kept] + land[level][j]
        if level + 1 < levels:
            part[j, kept] = total
            reduce_copy(level + 1, j).start()
        else:
            full[j, kept] = total
            gather_copy(level, j).start()

    def products(j, f, shots_at):
        first = full[j, pl.ds(2 * f * per, per)].reshape(rows, shots)[:, shots_at]
        second = full[j, pl.ds((2 * f + 1) * per, per)].reshape(rows, shots)[:, shots_at]
        both = jnp.concatenate(
            [recv[j, f, c].reshape(shots, receivers)[shots_at] for c in range(2)], axis=1
        )
        by_first = jnp.dot(first, both, preferred_element_type=jnp.float32)
        by_second = jnp.dot(second, both, preferred_element_type=jnp.float32)
        real = by_first[:, :receivers] + by_second[:, receivers:]
        imag = by_first[:, receivers:] - by_second[:, :receivers]
        return real, imag

    def store(at, pair):
        for c in range(2):
            out_ref[:, at, c] = (pair[c] * scale).reshape(rounds, SB, receivers).astype(jnp.bfloat16)

    def correlate_whole(j):
        for f in range(fs):
            store(whole_first(j) + f, products(j, f, slice(None)))

    def correlate_split(j):
        for f in range(fs):
            at = split_first(j) + f
            pair = products(j, f, slice(mid, None))
            for c in range(2):
                out_part[at, c] = pair[c].astype(jnp.bfloat16)
        partial_copy(j).start()
        for f in range(fs):
            at = split_first(j) + f
            pair = products(j, f, slice(0, mid))
            for c in range(2):
                acc[at, c] = pair[c]

    def correlate(j):
        by_kind(j, correlate_split, correlate_whole)

    def combine(j):
        partial_copy(j).wait_recv()
        for f in range(fs):
            at = split_first(j) + f
            store(at, [acc[at, c] + in_part[at, c].astype(jnp.float32) for c in range(2)])

    def gather(level, j):
        gather_copy(level, j, arrival=True).wait_recv()
        if level:
            gather_copy(level - 1, j).start()
        else:
            correlate(j)

    steps = [select]
    steps += [functools.partial(reduce, level) for level in range(levels)]
    steps += [functools.partial(gather, level) for level in reversed(range(levels))]

    last = SPACING * (len(steps) - 1) + LATER

    @pl.loop(0, stages + last)
    def _(tick):
        for place in reversed(range(len(steps))):
            j = tick - SPACING * place
            pl.when((j >= 0) & (j < stages))(functools.partial(steps[place], j))
        j = tick - last
        pl.when((j >= 0) & (j < stages) & is_split(j))(functools.partial(combine, j))

    def sent_split(j):
        for copy in split_sends(j) + [partial_copy(j)]:
            copy.wait_send()

    def sent_whole(j):
        for copy in whole_sends(j):
            copy.wait_send()

    @pl.loop(0, stages)
    def _(j):
        by_kind(j, sent_split, sent_whole)
        for level in range(levels):
            reduce_copy(level, j).wait_send()
            gather_copy(level, j).wait_send()


def body(spectra, source_block, taper_window):
    f_all, parts, shot_dev, node_dev = spectra.shape
    nodes = lax.axis_size("node")
    groups = lax.axis_size("shot")
    levels = nodes.bit_length() - 1
    rounds = source_block.shape[0]
    f_dev = f_all // groups
    shots = shot_dev * groups
    rows = rounds * SB
    fs = max(1, nodes // 8)
    stages = f_dev // fs
    unit = fs * parts * rows // nodes
    scale = 1.0 / float(shots) ** 0.5

    first = lax.axis_index("node") * node_dev
    picked = source_block[:, None] * SB + jnp.arange(SB, dtype=jnp.int32)[None, :] - first
    sel = (picked.reshape(rows, 1) == jnp.arange(node_dev, dtype=jnp.int32)[None, :]).astype(jnp.bfloat16)
    weights = taper_weights(taper_window)
    here = lax.axis_index("shot") // (groups // 2) * (shots // 2)
    weights_here = lax.dynamic_slice_in_dim(weights, here, shots // 2, 1)
    weights = jnp.stack((weights, jnp.concatenate((weights_here, weights_here), axis=1)))

    bf = jnp.bfloat16
    dma = pltpu.SemaphoreType.DMA
    return pl.pallas_call(
        functools.partial(kernel, nodes, groups, stages, scale),
        out_shape=jax.ShapeDtypeStruct((rounds, f_dev, parts, SB, node_dev), bf),
        in_specs=[
            pl.BlockSpec(memory_space=pltpu.VMEM),
            pl.BlockSpec(memory_space=pltpu.VMEM),
            pl.BlockSpec(memory_space=pl.ANY),
        ],
        out_specs=pl.BlockSpec(memory_space=pltpu.VMEM),
        scratch_shapes=[
            pltpu.VMEM((stages, fs, parts, groups, shot_dev, node_dev), bf),
            pltpu.VMEM((stages, nodes, unit, shots), bf),
            pltpu.VMEM((stages, nodes, unit, shots), bf),
            pltpu.VMEM((f_dev // 2, parts, rows, node_dev), jnp.float32),
            pltpu.VMEM((f_dev // 2, parts, rows, node_dev), bf),
            pltpu.VMEM((f_dev // 2, parts, rows, node_dev), bf),
            *[pltpu.VMEM((stages, nodes >> (level + 1), unit, shots), bf) for level in range(levels)],
            dma((stages, 2)),
            dma((stages, groups - 1)),
            dma((stages, groups - 1)),
            dma((levels, stages)),
            dma((levels, stages)),
            dma((levels, stages)),
            dma((levels, stages)),
            dma((stages,)),
            dma((stages,)),
        ],
        compiler_params=pltpu.CompilerParams(
            collective_id=0, has_side_effects=True, vmem_limit_bytes=48 * 1024 * 1024
        ),
        cost_estimate=pl.CostEstimate(
            flops=2 * 5 * f_dev * rows * shots * node_dev * 2, bytes_accessed=spectra.size * 4, transcendentals=0
        ),
    )(sel, weights, spectra)


def solution(mesh):
    in_specs = (P(None, None, "shot", "node"), P(), P())
    out_specs = P(None, "shot", None, None, "node")
    return jax.shard_map(body, mesh=mesh, in_specs=in_specs, out_specs=out_specs, check_vma=False)
```

time: 128 us -> 104 us (0.81); the launches traced: 125 us -> 103 us
  Pallas kernels: 120 us -> 97.7 us
    pallas_call x1, Pallas kernels: 120 us -> 97.7 us  [body(): pl.pallas_call(functools.partial(kernel, nodes, groups, stages, scale), o...]
where the time goes in v4:
time: 104 us; the launch traced here: 103 us
  Pallas kernels  97.7 us (94%)
  local copies, waits for them, and re-layouts  3.42 us (3%)
  other arithmetic  1.62 us (2%)
    pallas_call x1, Pallas kernels, body(): pl.pallas_call(functools.partial(kernel, nodes, groups, stages, scale), o...  97.7 us
    unnamed x3, local copies, waits for them, and re-layouts  3.33 us

profile of v4, /device:TPU:0, one launch (start us, length us, event | category | flops | bytes accessed | tf_op | source)
XLA Modules:
  0.0 102.8 jit_solution(17366073585073128788)
XLA Ops:
  0.0 0.7 broadcast_multiply_fusion
  0.7 0.1 add_subtract_fusion
  0.7 0.1 sub.22
  0.8 0.8 fusion.1
  1.7 0.1 fusion.sel_ref
  1.7 0.0 copy-start
  1.8 2.2 %copy-done = bf16[64,2,128,128]{3,2,1,0:T(8,128)(2,1)S(1)} copy-done((bf16[64,2,128,128]{3,2,1,0:T(8,128)(2,1)S(1)}, bf16[64,2,128,128]{3,2,1,0:T(8,128)(2,1)}, u32[]{:S(2)}) %copy-start) | copy-done | bytes 4194328
  3.9 97.7 %shard_map.37 = bf16[6,16,2,32,128]{4,3,2,1,0:T(8,128)(2,1)S(1)} custom-call(bf16[192,128]{1,0:T(8,128)(2,1)S(1)} %fusion.sel_ref, f32[2,6,512]{2,1,0:T(8,128)S(1)} %pad_maximum_fusion.weight_ref, bf16[64,2,128,128]{3,2,1,0:T(8,128)(2,1)S(1)} %copy-done), custom_call_target="tpu_custom_call" | custom-call | flops 4026531840 | bytes 8388608 | tf_op jit(solution)/shard_map/pallas_call | solution.py:343
  101.6 1.1 %copy.5 = bf16[6,16,2,32,128]{4,3,2,1,0:T(8,128)(2,1)} copy(bf16[6,16,2,32,128]{4,3,2,1,0:T(8,128)(2,1)S(1)} %shard_map.37) | data formatting | bytes 3145728
  (3 shorter events, 0.0 us)
Async XLA Ops:
  1.7 2.2 %copy-start = (bf16[64,2,128,128]{3,2,1,0:T(8,128)(2,1)S(1)}, bf16[64,2,128,128]{3,2,1,0:T(8,128)(2,1)}, u32[]{:S(2)}) copy-start(bf16[64,2,128,128]{3,2,1,0:T(8,128)(2,1)} %x_ref.1) | copy-start | bytes 12582916

commit v5 on v4

--- a/solution.py
+++ b/solution.py
@@ -10,7 +10,7 @@
 SB = 32
 WINDOWS = 8
 MESH = pl.DeviceIdType.MESH
-AHEAD = 6
+AHEAD = 16
 SPACING = 2
 LATER = 5
 
@@ -21,8 +21,8 @@
 
 def kernel(
     nodes, groups, stages, scale,
-    sel_ref, weight_ref, x_ref, out_ref,
-    recv, part, full, acc, out_part, in_part, *rest,
+    block_ref, window_ref, x_ref, out_ref,
+    sel_ref, weight_ref, recv, part, full, acc, out_part, in_part, *rest,
 ):
     levels = nodes.bit_length() - 1
     land = rest[:levels]
@@ -194,6 +194,17 @@
     def _(j):
         by_kind(j, start_split, start_whole)
 
+    for r in range(rounds):
+        at = block_ref[r] * SB - me * receivers
+        column = lax.broadcasted_iota(jnp.int32, (SB, receivers), 1)
+        row = lax.broadcasted_iota(jnp.int32, (SB, receivers), 0)
+        sel_ref[pl.ds(r * SB, SB)] = jnp.where(column == row + at, 1.0, 0.0).astype(jnp.bfloat16)
+    weights = taper_weights(window_ref[...])
+    low, high = weights[:, :mid], weights[:, mid:]
+    here = jnp.where(side == 0, low, high)
+    weight_ref[0] = weights
+    weight_ref[1] = jnp.concatenate((here, here), axis=1)
+
     def pick(j, kind):
         for f in range(fs):
             for c in range(2):
@@ -330,26 +341,20 @@
     unit = fs * parts * rows // nodes
     scale = 1.0 / float(shots) ** 0.5
 
-    first = lax.axis_index("node") * node_dev
-    picked = source_block[:, None] * SB + jnp.arange(SB, dtype=jnp.int32)[None, :] - first
-    sel = (picked.reshape(rows, 1) == jnp.arange(node_dev, dtype=jnp.int32)[None, :]).astype(jnp.bfloat16)
-    weights = taper_weights(taper_window)
-    here = lax.axis_index("shot") // (groups // 2) * (shots // 2)
-    weights_here = lax.dynamic_slice_in_dim(weights, here, shots // 2, 1)
-    weights = jnp.stack((weights, jnp.concatenate((weights_here, weights_here), axis=1)))
-
     bf = jnp.bfloat16
     dma = pltpu.SemaphoreType.DMA
     return pl.pallas_call(
         functools.partial(kernel, nodes, groups, stages, scale),
         out_shape=jax.ShapeDtypeStruct((rounds, f_dev, parts, SB, node_dev), bf),
         in_specs=[
-            pl.BlockSpec(memory_space=pltpu.VMEM),
+            pl.BlockSpec(memory_space=pltpu.SMEM),
             pl.BlockSpec(memory_space=pltpu.VMEM),
             pl.BlockSpec(memory_space=pl.ANY),
         ],
         out_specs=pl.BlockSpec(memory_space=pltpu.VMEM),
         scratch_shapes=[
+            pltpu.VMEM((rows, node_dev), bf),
+            pltpu.VMEM((2, rounds, shots), jnp.float32),
             pltpu.VMEM((stages, fs, parts, groups, shot_dev, node_dev), bf),
             pltpu.VMEM((stages, nodes, unit, shots), bf),
             pltpu.VMEM((stages, nodes, unit, shots), bf),
@@ -368,12 +373,12 @@
             dma((stages,)),
         ],
         compiler_params=pltpu.CompilerParams(
-            collective_id=0, has_side_effects=True, vmem_limit_bytes=48 * 1024 * 1024
+            collective_id=0, has_side_effects=True, vmem_limit_bytes=51 * 1024 * 1024
         ),
         cost_estimate=pl.CostEstimate(
             flops=2 * 5 * f_dev * rows * shots * node_dev * 2, bytes_accessed=spectra.size * 4, transcendentals=0
         ),
-    )(sel, weights, spectra)
+    )(source_block, taper_window, spectra)
 
 
 def solution(mesh):

time: 104 us -> 102 us (0.981)
  other arithmetic: 1.62 us -> 0 us
    unnamed x3 -> x5, local copies, waits for them, and re-layouts: 3.33 us -> 2.52 us
where the time goes in v5:
time: 102 us; the launch traced here: 101 us
  Pallas kernels  98.6 us (97%)
  local copies, waits for them, and re-layouts  2.52 us (2%)
    pallas_call x1, Pallas kernels, body(): pl.pallas_call(functools.partial(kernel, nodes, groups, stages, scale), o...  98.6 us
    unnamed x5, local copies, waits for them, and re-layouts  2.52 us

profile of v5, /device:TPU:0, one launch (start us, length us, event | category | flops | bytes accessed | tf_op | source)
XLA Modules:
  0.0 101.1 jit_solution(5981866552344426837)
XLA Ops:
  0.0 0.0 copy-start
  0.0 0.7 copy-done
  0.7 0.0 copy-start.1
  0.7 0.7 copy-done.1
  1.4 98.6 %shard_map.37 = bf16[6,16,2,32,128]{4,3,2,1,0:T(8,128)(2,1)S(1)} custom-call(s32[6]{0:T(128)S(1)} %copy-done.1, s32[6,512]{1,0:T(8,128)S(1)} %copy-done, bf16[64,2,128,128]{3,2,1,0:T(8,128)(2,1)} %x_ref.1), custom_call_target="tpu_custom_call" | custom-call | flops 4026531840 | bytes 8388608 | tf_op jit(solution)/shard_map/pallas_call | solution.py:346
  99.9 1.1 %copy.5 = bf16[6,16,2,32,128]{4,3,2,1,0:T(8,128)(2,1)} copy(bf16[6,16,2,32,128]{4,3,2,1,0:T(8,128)(2,1)S(1)} %shard_map.37) | data formatting | bytes 3145728
Async XLA Ops:
  0.0 0.7 copy-start
  0.7 0.7 copy-start.1

commit v6 on v5

--- a/solution.py
+++ b/solution.py
@@ -12,7 +12,7 @@
 MESH = pl.DeviceIdType.MESH
 AHEAD = 16
 SPACING = 2
-LATER = 5
+LATER = 9
 
 
 def taper_weights(taper_windows):
@@ -305,7 +305,7 @@
 
     @pl.loop(0, stages + last)
     def _(tick):
-        for place in reversed(range(len(steps))):
+        for place in [*reversed(range(1, len(steps) - 1)), len(steps) - 1, 0]:
             j = tick - SPACING * place
             pl.when((j >= 0) & (j < stages))(functools.partial(steps[place], j))
         j = tick - last

time: 102 us -> 102 us (level)
  no operation moved by 1% of the time
where the time goes in v6:
time: 102 us
  Pallas kernels  99.2 us (97%)
  local copies, waits for them, and re-layouts  2.52 us (2%)
    pallas_call x1, Pallas kernels, body(): pl.pallas_call(functools.partial(kernel, nodes, groups, stages, scale), o...  99.2 us
    unnamed x5, local copies, waits for them, and re-layouts  2.52 us

profile of v6, /device:TPU:0, one launch (start us, length us, event | category | flops | bytes accessed | tf_op | source)
XLA Modules:
  0.0 101.7 jit_solution(3983916909807884637)
XLA Ops:
  0.0 0.0 copy-start
  0.0 0.7 copy-done
  0.7 0.0 copy-start.1
  0.7 0.7 copy-done.1
  1.4 99.2 %shard_map.37 = bf16[6,16,2,32,128]{4,3,2,1,0:T(8,128)(2,1)S(1)} custom-call(s32[6]{0:T(128)S(1)} %copy-done.1, s32[6,512]{1,0:T(8,128)S(1)} %copy-done, bf16[64,2,128,128]{3,2,1,0:T(8,128)(2,1)} %x_ref.1), custom_call_target="tpu_custom_call" | custom-call | flops 4026531840 | bytes 8388608 | tf_op jit(solution)/shard_map/pallas_call | solution.py:346
  100.6 1.1 %copy.5 = bf16[6,16,2,32,128]{4,3,2,1,0:T(8,128)(2,1)} copy(bf16[6,16,2,32,128]{4,3,2,1,0:T(8,128)(2,1)S(1)} %shard_map.37) | data formatting | bytes 3145728
Async XLA Ops:
  0.0 0.7 copy-start
  0.7 0.7 copy-start.1

commit v7 on v6

--- a/solution.py
+++ b/solution.py
@@ -32,9 +32,10 @@
     half = groups // 2
     side, rank = group // half, group % half
     counterpart = (1 - side) * half + rank
-    fs = recv.shape[1]
+    fs = recv.shape[2]
     f_dev = stages * fs
-    halves = stages // 2
+    splits = acc.shape[0] // fs
+    wholes = stages - splits
     mid = part.shape[-1] // 2
     rows = sel_ref.shape[0]
     shots = part.shape[-1]
@@ -62,14 +63,17 @@
             at = at + hop(lower, j)[0] * (nodes >> (lower + 1))
         return at
 
+    def wholes_before(j):
+        return j * (wholes - 1) // (stages - 1)
+
     def is_split(j):
-        return (j == 0) | ((j % 2 == 1) & (j < stages - 1))
+        return (j < stages - 1) & (wholes_before(j + 1) == wholes_before(j))
 
     def split_first(j):
-        return (j + 1) // 2 * fs
+        return (j - wholes_before(j)) * fs
 
     def whole_first(j):
-        return (halves + (j + 1) // 2 - 1) * fs
+        return (splits + wholes_before(j)) * fs
 
     def frequencies(owner, first):
         return x_ref.at[pl.ds(owner * f_dev + first, fs)]
@@ -77,7 +81,7 @@
     def send(j, number, source, slot, to):
         return pltpu.make_async_remote_copy(
             src_ref=source,
-            dst_ref=recv.at[j, :, :, slot],
+            dst_ref=recv.at[j, slot],
             send_sem=zs.at[j, number],
             recv_sem=zr.at[j, number],
             device_id=(me, to),
@@ -96,7 +100,7 @@
         out = []
         for d in range(1, groups):
             source = (group + groups - d) % groups
-            out.append(send(j, d - 1, recv.at[j, :, :, source], source, source))
+            out.append(send(j, d - 1, recv.at[j, source], source, source))
         return out
 
     def split_sends(j):
@@ -117,19 +121,19 @@
             source = (rank + half - d) % half
             for other in range(2):
                 place = other * half + source
-                out.append(send(j, 2 * (d - 1) + other, recv.at[j, :, :, place], place, side * half + source))
+                out.append(send(j, 2 * (d - 1) + other, recv.at[j, place], place, side * half + source))
         return out
 
     def whole_own(j):
         return [
-            pltpu.make_async_copy(frequencies(group, whole_first(j)), recv.at[j, :, :, group], own_sem.at[j, 0])
+            pltpu.make_async_copy(frequencies(group, whole_first(j)), recv.at[j, group], own_sem.at[j, 0])
         ]
 
     def split_own(j):
         return [
-            pltpu.make_async_copy(frequencies(group, split_first(j)), recv.at[j, :, :, rank], own_sem.at[j, 0]),
+            pltpu.make_async_copy(frequencies(group, split_first(j)), recv.at[j, rank], own_sem.at[j, 0]),
             pltpu.make_async_copy(
-                frequencies(counterpart, split_first(j)), recv.at[j, :, :, half + rank], own_sem.at[j, 1]
+                frequencies(counterpart, split_first(j)), recv.at[j, half + rank], own_sem.at[j, 1]
             ),
         ]
 
@@ -208,7 +212,7 @@
     def pick(j, kind):
         for f in range(fs):
             for c in range(2):
-                block = recv[j, f, c].reshape(shots, receivers)
+                block = recv[j, :, f, c].reshape(shots, receivers)
                 picked = lax.dot_general(
                     sel_ref[...], block, (((1,), (1,)), ((), ())),
                     preferred_element_type=jnp.float32,
@@ -252,7 +256,7 @@
         first = full[j, pl.ds(2 * f * per, per)].reshape(rows, shots)[:, shots_at]
         second = full[j, pl.ds((2 * f + 1) * per, per)].reshape(rows, shots)[:, shots_at]
         both = jnp.concatenate(
-            [recv[j, f, c].reshape(shots, receivers)[shots_at] for c in range(2)], axis=1
+            [recv[j, :, f, c].reshape(shots, receivers)[shots_at] for c in range(2)], axis=1
         )
         by_first = jnp.dot(first, both, preferred_element_type=jnp.float32)
         by_second = jnp.dot(second, both, preferred_element_type=jnp.float32)
@@ -338,6 +342,7 @@
     rows = rounds * SB
     fs = max(1, nodes // 8)
     stages = f_dev // fs
+    splits = max(1, stages * 5 // 8)
     unit = fs * parts * rows // nodes
     scale = 1.0 / float(shots) ** 0.5
 
@@ -355,12 +360,12 @@
         scratch_shapes=[
             pltpu.VMEM((rows, node_dev), bf),
             pltpu.VMEM((2, rounds, shots), jnp.float32),
-            pltpu.VMEM((stages, fs, parts, groups, shot_dev, node_dev), bf),
+            pltpu.VMEM((stages, groups, fs, parts, shot_dev, node_dev), bf),
             pltpu.VMEM((stages, nodes, unit, shots), bf),
             pltpu.VMEM((stages, nodes, unit, shots), bf),
-            pltpu.VMEM((f_dev // 2, parts, rows, node_dev), jnp.float32),
-            pltpu.VMEM((f_dev // 2, parts, rows, node_dev), bf),
-            pltpu.VMEM((f_dev // 2, parts, rows, node_dev), bf),
+            pltpu.VMEM((splits * fs, parts, rows, node_dev), jnp.float32),
+            pltpu.VMEM((splits * fs, parts, rows, node_dev), bf),
+            pltpu.VMEM((splits * fs, parts, rows, node_dev), bf),
             *[pltpu.VMEM((stages, nodes >> (level + 1), unit, shots), bf) for level in range(levels)],
             dma((stages, 2)),
             dma((stages, groups - 1)),

time: 102 us -> 104 us (1.020)
  Pallas kernels: 99.2 us -> 102 us
    pallas_call x1, Pallas kernels: 99.2 us -> 102 us  [body(): pl.pallas_call(functools.partial(kernel, nodes, groups, stages, scale), o...]
where the time goes in v7:
time: 104 us
  Pallas kernels  102 us (98%)
  local copies, waits for them, and re-layouts  2.52 us (2%)
    pallas_call x1, Pallas kernels, body(): pl.pallas_call(functools.partial(kernel, nodes, groups, stages, scale), o...  102 us
    unnamed x5, local copies, waits for them, and re-layouts  2.52 us

profile of v7, /device:TPU:0, one launch (start us, length us, event | category | flops | bytes accessed | tf_op | source)
XLA Modules:
  0.0 104.2 jit_solution(13707677880833620898)
XLA Ops:
  0.0 0.0 copy-start
  0.0 0.7 copy-done
  0.7 0.0 copy-start.1
  0.7 0.7 copy-done.1
  1.4 101.6 %shard_map.37 = bf16[6,16,2,32,128]{4,3,2,1,0:T(8,128)(2,1)S(1)} custom-call(s32[6]{0:T(128)S(1)} %copy-done.1, s32[6,512]{1,0:T(8,128)S(1)} %copy-done, bf16[64,2,128,128]{3,2,1,0:T(8,128)(2,1)} %x_ref.1), custom_call_target="tpu_custom_call" | custom-call | flops 4026531840 | bytes 8388608 | tf_op jit(solution)/shard_map/pallas_call | solution.py:351
  103.0 1.1 %copy.5 = bf16[6,16,2,32,128]{4,3,2,1,0:T(8,128)(2,1)} copy(bf16[6,16,2,32,128]{4,3,2,1,0:T(8,128)(2,1)S(1)} %shard_map.37) | data formatting | bytes 3145728
Async XLA Ops:
  0.0 0.7 copy-start
  0.7 0.7 copy-start.1

commit v8 on v7

--- a/solution.py
+++ b/solution.py
@@ -11,8 +11,8 @@
 WINDOWS = 8
 MESH = pl.DeviceIdType.MESH
 AHEAD = 16
-SPACING = 2
-LATER = 9
+SPACING = 3
+LATER = 6
 
 
 def taper_weights(taper_windows):
@@ -342,7 +342,7 @@
     rows = rounds * SB
     fs = max(1, nodes // 8)
     stages = f_dev // fs
-    splits = max(1, stages * 5 // 8)
+    splits = stages // 2
     unit = fs * parts * rows // nodes
     scale = 1.0 / float(shots) ** 0.5
 

time: 104 us -> 110 us (1.058)
  Pallas kernels: 102 us -> 107 us
    pallas_call x1, Pallas kernels: 102 us -> 107 us  [body(): pl.pallas_call(functools.partial(kernel, nodes, groups, stages, scale), o...]
where the time goes in v8:
time: 110 us; the launch traced here: 109 us
  Pallas kernels  107 us (97%)
  local copies, waits for them, and re-layouts  2.52 us (2%)
    pallas_call x1, Pallas kernels, body(): pl.pallas_call(functools.partial(kernel, nodes, groups, stages, scale), o...  107 us
    unnamed x5, local copies, waits for them, and re-layouts  2.52 us

profile of v8, /device:TPU:0, one launch (start us, length us, event | category | flops | bytes accessed | tf_op | source)
XLA Modules:
  0.0 109.3 jit_solution(13240556590648298603)
XLA Ops:
  0.0 0.0 copy-start
  0.0 0.7 copy-done
  0.7 0.0 copy-start.1
  0.7 0.7 copy-done.1
  1.4 106.8 %shard_map.37 = bf16[6,16,2,32,128]{4,3,2,1,0:T(8,128)(2,1)S(1)} custom-call(s32[6]{0:T(128)S(1)} %copy-done.1, s32[6,512]{1,0:T(8,128)S(1)} %copy-done, bf16[64,2,128,128]{3,2,1,0:T(8,128)(2,1)} %x_ref.1), custom_call_target="tpu_custom_call" | custom-call | flops 4026531840 | bytes 8388608 | tf_op jit(solution)/shard_map/pallas_call | solution.py:351
  108.1 1.1 %copy.5 = bf16[6,16,2,32,128]{4,3,2,1,0:T(8,128)(2,1)} copy(bf16[6,16,2,32,128]{4,3,2,1,0:T(8,128)(2,1)S(1)} %shard_map.37) | data formatting | bytes 3145728
Async XLA Ops:
  0.0 0.7 copy-start
  0.7 0.7 copy-start.1

commit v9 on v8

--- a/solution.py
+++ b/solution.py
@@ -11,7 +11,6 @@
 WINDOWS = 8
 MESH = pl.DeviceIdType.MESH
 AHEAD = 16
-SPACING = 3
 LATER = 6
 
 
@@ -305,12 +304,15 @@
     steps += [functools.partial(reduce, level) for level in range(levels)]
     steps += [functools.partial(gather, level) for level in reversed(range(levels))]
 
-    last = SPACING * (len(steps) - 1) + LATER
+    at_tick = [0]
+    for step in range(1, len(steps)):
+        at_tick.append(at_tick[-1] + (1 if step in (1, levels, levels + 1, 2 * levels) else 2))
+    last = at_tick[-1] + LATER
 
     @pl.loop(0, stages + last)
     def _(tick):
         for place in [*reversed(range(1, len(steps) - 1)), len(steps) - 1, 0]:
-            j = tick - SPACING * place
+            j = tick - at_tick[place]
             pl.when((j >= 0) & (j < stages))(functools.partial(steps[place], j))
         j = tick - last
         pl.when((j >= 0) & (j < stages) & is_split(j))(functools.partial(combine, j))

time: 110 us -> 113 us (1.027)
  Pallas kernels: 107 us -> 110 us
    pallas_call x1, Pallas kernels: 107 us -> 110 us  [body(): pl.pallas_call(functools.partial(kernel, nodes, groups, stages, scale), o...]
where the time goes in v9:
time: 113 us
  Pallas kernels  110 us (97%)
  local copies, waits for them, and re-layouts  2.52 us (2%)
    pallas_call x1, Pallas kernels, body(): pl.pallas_call(functools.partial(kernel, nodes, groups, stages, scale), o...  110 us
    unnamed x5, local copies, waits for them, and re-layouts  2.52 us

profile of v9, /device:TPU:0, one launch (start us, length us, event | category | flops | bytes accessed | tf_op | source)
XLA Modules:
  0.0 112.5 jit_solution(10142126617887175455)
XLA Ops:
  0.0 0.0 copy-start
  0.0 0.7 copy-done
  0.7 0.0 copy-start.1
  0.7 0.7 copy-done.1
  1.4 110.0 %shard_map.37 = bf16[6,16,2,32,128]{4,3,2,1,0:T(8,128)(2,1)S(1)} custom-call(s32[6]{0:T(128)S(1)} %copy-done.1, s32[6,512]{1,0:T(8,128)S(1)} %copy-done, bf16[64,2,128,128]{3,2,1,0:T(8,128)(2,1)} %x_ref.1), custom_call_target="tpu_custom_call" | custom-call | flops 4026531840 | bytes 8388608 | tf_op jit(solution)/shard_map/pallas_call | solution.py:353
  111.4 1.1 %copy.5 = bf16[6,16,2,32,128]{4,3,2,1,0:T(8,128)(2,1)} copy(bf16[6,16,2,32,128]{4,3,2,1,0:T(8,128)(2,1)S(1)} %shard_map.37) | data formatting | bytes 3145728
Async XLA Ops:
  0.0 0.7 copy-start
  0.7 0.7 copy-start.1

commit v10 on v5

--- a/solution.py
+++ b/solution.py
@@ -13,6 +13,7 @@
 AHEAD = 16
 SPACING = 2
 LATER = 5
+PIECES = 2
 
 
 def taper_weights(taper_windows):
@@ -149,31 +150,48 @@
         pl.when(split)(functools.partial(on_split, j))
         pl.when(jnp.logical_not(split))(functools.partial(on_whole, j))
 
-    def reduce_copy(level, j):
+    def pieces(level):
+        size = nodes >> (level + 1)
+        count = PIECES if level == 0 else 1
+        return [(n, n * size // count, size // count) for n in range(count)]
+
+    def reduce_copies(level, j):
         bit, peer = hop(level, j)
-        size = nodes >> (level + 1)
-        return pltpu.make_async_remote_copy(
-            src_ref=part.at[j, pl.ds(offset(level, j) + (1 - bit) * size, size)],
-            dst_ref=land[level].at[j],
-            send_sem=rs.at[level, j],
-            recv_sem=rr.at[level, j],
-            device_id=(peer, group),
-            device_id_type=MESH,
-        )
-
-    def gather_copy(level, j, arrival=False):
+        start = offset(level, j) + (1 - bit) * (nodes >> (level + 1))
+        return [
+            pltpu.make_async_remote_copy(
+                src_ref=part.at[j, pl.ds(start + at, size)],
+                dst_ref=land[level].at[j, pl.ds(at, size)],
+                send_sem=rs.at[level, j, n],
+                recv_sem=rr.at[level, j, n],
+                device_id=(peer, group),
+                device_id_type=MESH,
+            )
+            for n, at, size in pieces(level)
+        ]
+
+    def gather_copies(level, j, arrival=False):
         bit, peer = hop(level, j)
-        size = nodes >> (level + 1)
         side_at = 1 - bit if arrival else bit
-        place = full.at[j, pl.ds(offset(level, j) + side_at * size, size)]
-        return pltpu.make_async_remote_copy(
-            src_ref=place,
-            dst_ref=place,
-            send_sem=gs.at[level, j],
-            recv_sem=gr.at[level, j],
-            device_id=(peer, group),
-            device_id_type=MESH,
-        )
+        start = offset(level, j) + side_at * (nodes >> (level + 1))
+        out = []
+        for n, at, size in pieces(level):
+            place = full.at[j, pl.ds(start + at, size)]
+            out.append(
+                pltpu.make_async_remote_copy(
+                    src_ref=place,
+                    dst_ref=place,
+                    send_sem=gs.at[level, j, n],
+                    recv_sem=gr.at[level, j, n],
+                    device_id=(peer, group),
+                    device_id_type=MESH,
+                )
+            )
+        return out
+
+    def start_all(copies):
+        for copy in copies:
+            copy.start()
 
     barrier = pltpu.get_barrier_semaphore()
     for level in range(levels):
@@ -233,20 +251,21 @@
     def select(j):
         pl.when(j + AHEAD < stages)(lambda: by_kind(j + AHEAD, start_split, start_whole))
         by_kind(j, select_split, select_whole)
-        reduce_copy(0, j).start()
+        start_all(reduce_copies(0, j))
 
     def reduce(level, j):
-        reduce_copy(level, j).wait_recv()
+        for copy in reduce_copies(level, j):
+            copy.wait_recv()
         bit, _ = hop(level, j)
         size = nodes >> (level + 1)
         kept = pl.ds(offset(level, j) + bit * size, size)
         total = part[j, kept] + land[level][j]
         if level + 1 < levels:
             part[j, kept] = total
-            reduce_copy(level + 1, j).start()
+            start_all(reduce_copies(level + 1, j))
         else:
             full[j, kept] = total
-            gather_copy(level, j).start()
+            start_all(gather_copies(level, j))
 
     def products(j, f, shots_at):
         first = full[j, pl.ds(2 * f * per, per)].reshape(rows, shots)[:, shots_at]
@@ -291,9 +310,10 @@
             store(at, [acc[at, c] + in_part[at, c].astype(jnp.float32) for c in range(2)])
 
     def gather(level, j):
-        gather_copy(level, j, arrival=True).wait_recv()
+        for copy in gather_copies(level, j, arrival=True):
+            copy.wait_recv()
         if level:
-            gather_copy(level - 1, j).start()
+            start_all(gather_copies(level - 1, j))
         else:
             correlate(j)
 
@@ -323,8 +343,8 @@
     def _(j):
         by_kind(j, sent_split, sent_whole)
         for level in range(levels):
-            reduce_copy(level, j).wait_send()
-            gather_copy(level, j).wait_send()
+            for copy in reduce_copies(level, j) + gather_copies(level, j):
+                copy.wait_send()
 
 
 def body(spectra, source_block, taper_window):
@@ -365,10 +385,10 @@
             dma((stages, 2)),
             dma((stages, groups - 1)),
             dma((stages, groups - 1)),
-            dma((levels, stages)),
-            dma((levels, stages)),
-            dma((levels, stages)),
-            dma((levels, stages)),
+            dma((levels, stages, PIECES)),
+            dma((levels, stages, PIECES)),
+            dma((levels, stages, PIECES)),
+            dma((levels, stages, PIECES)),
             dma((stages,)),
             dma((stages,)),
         ],

time: 102 us -> 104 us (1.020)
  Pallas kernels: 98.6 us -> 100 us
    pallas_call x1, Pallas kernels: 98.6 us -> 100 us  [body(): pl.pallas_call(functools.partial(kernel, nodes, groups, stages, scale), o...]
where the time goes in v10:
time: 104 us; the launch traced here: 103 us
  Pallas kernels  100 us (96%)
  local copies, waits for them, and re-layouts  2.52 us (2%)
    pallas_call x1, Pallas kernels, body(): pl.pallas_call(functools.partial(kernel, nodes, groups, stages, scale), o...  100 us
    unnamed x5, local copies, waits for them, and re-layouts  2.52 us

profile of v10, /device:TPU:0, one launch (start us, length us, event | category | flops | bytes accessed | tf_op | source)
XLA Modules:
  0.0 102.9 jit_solution(16539124834016534666)
XLA Ops:
  0.0 0.0 copy-start
  0.0 0.7 copy-done
  0.7 0.0 copy-start.1
  0.7 0.7 copy-done.1
  1.4 100.4 %shard_map.37 = bf16[6,16,2,32,128]{4,3,2,1,0:T(8,128)(2,1)S(1)} custom-call(s32[6]{0:T(128)S(1)} %copy-done.1, s32[6,512]{1,0:T(8,128)S(1)} %copy-done, bf16[64,2,128,128]{3,2,1,0:T(8,128)(2,1)} %x_ref.1), custom_call_target="tpu_custom_call" | custom-call | flops 4026531840 | bytes 8388608 | tf_op jit(solution)/shard_map/pallas_call | solution.py:366
  101.7 1.1 %copy.5 = bf16[6,16,2,32,128]{4,3,2,1,0:T(8,128)(2,1)} copy(bf16[6,16,2,32,128]{4,3,2,1,0:T(8,128)(2,1)S(1)} %shard_map.37) | data formatting | bytes 3145728
Async XLA Ops:
  0.0 0.7 copy-start
  0.7 0.7 copy-start.1

commit v11 on v5

--- a/solution.py
+++ b/solution.py
@@ -10,7 +10,7 @@
 SB = 32
 WINDOWS = 8
 MESH = pl.DeviceIdType.MESH
-AHEAD = 16
+AHEAD = 3
 SPACING = 2
 LATER = 5
 

time: 102 us -> 101 us (level)
  no operation moved by 1% of the time
where the time goes in v11:
time: 101 us
  Pallas kernels  98.5 us (98%)
  local copies, waits for them, and re-layouts  2.52 us (2%)
    pallas_call x1, Pallas kernels, body(): pl.pallas_call(functools.partial(kernel, nodes, groups, stages, scale), o...  98.5 us
    unnamed x5, local copies, waits for them, and re-layouts  2.52 us

profile of v11, /device:TPU:0, one launch (start us, length us, event | category | flops | bytes accessed | tf_op | source)
XLA Modules:
  0.0 101.0 jit_solution(7249263048650512680)
XLA Ops:
  0.0 0.0 copy-start
  0.0 0.7 copy-done
  0.7 0.0 copy-start.1
  0.7 0.7 copy-done.1
  1.4 98.5 %shard_map.37 = bf16[6,16,2,32,128]{4,3,2,1,0:T(8,128)(2,1)S(1)} custom-call(s32[6]{0:T(128)S(1)} %copy-done.1, s32[6,512]{1,0:T(8,128)S(1)} %copy-done, bf16[64,2,128,128]{3,2,1,0:T(8,128)(2,1)} %x_ref.1), custom_call_target="tpu_custom_call" | custom-call | flops 4026531840 | bytes 8388608 | tf_op jit(solution)/shard_map/pallas_call | solution.py:346
  99.8 1.1 %copy.5 = bf16[6,16,2,32,128]{4,3,2,1,0:T(8,128)(2,1)} copy(bf16[6,16,2,32,128]{4,3,2,1,0:T(8,128)(2,1)S(1)} %shard_map.37) | data formatting | bytes 3145728
Async XLA Ops:
  0.0 0.7 copy-start
  0.7 0.7 copy-start.1

commit v12 on v11

--- a/solution.py
+++ b/solution.py
@@ -12,7 +12,7 @@
 MESH = pl.DeviceIdType.MESH
 AHEAD = 3
 SPACING = 2
-LATER = 5
+LATER = 9
 
 
 def taper_weights(taper_windows):

time: 101 us -> 101 us (level)
  no operation moved by 1% of the time
where the time goes in v12:
time: 101 us
  Pallas kernels  98.5 us (98%)
  local copies, waits for them, and re-layouts  2.52 us (2%)
    pallas_call x1, Pallas kernels, body(): pl.pallas_call(functools.partial(kernel, nodes, groups, stages, scale), o...  98.5 us
    unnamed x5, local copies, waits for them, and re-layouts  2.52 us

profile of v12, /device:TPU:0, one launch (start us, length us, event | category | flops | bytes accessed | tf_op | source)
XLA Modules:
  0.0 101.0 jit_solution(16364171398673784543)
XLA Ops:
  0.0 0.0 copy-start
  0.0 0.7 copy-done
  0.7 0.0 copy-start.1
  0.7 0.7 copy-done.1
  1.4 98.5 %shard_map.37 = bf16[6,16,2,32,128]{4,3,2,1,0:T(8,128)(2,1)S(1)} custom-call(s32[6]{0:T(128)S(1)} %copy-done.1, s32[6,512]{1,0:T(8,128)S(1)} %copy-done, bf16[64,2,128,128]{3,2,1,0:T(8,128)(2,1)} %x_ref.1), custom_call_target="tpu_custom_call" | custom-call | flops 4026531840 | bytes 8388608 | tf_op jit(solution)/shard_map/pallas_call | solution.py:346
  99.8 1.1 %copy.5 = bf16[6,16,2,32,128]{4,3,2,1,0:T(8,128)(2,1)} copy(bf16[6,16,2,32,128]{4,3,2,1,0:T(8,128)(2,1)S(1)} %shard_map.37) | data formatting | bytes 3145728
Async XLA Ops:
  0.0 0.7 copy-start
  0.7 0.7 copy-start.1
